TPU v7x, 32 devices: a whole 2x2x4 slice. The times are simulated.
32 devices in a mesh: rhs: 16 (over z, x, core), fac: 2 (over y).
Axes of the slice: x: 2, y: 2, z: 4, core: 2. Of those that a mesh axis runs over, the one named last changes fastest.
Arguments:
- right_sides: bfloat16 [1024, 768], P('rhs', 'fac'), may hold values from -6 to 6
- stripe: bfloat16 [768, 768], P('fac', 'rhs'), may hold values from -0.109375 to 0.109375
- inverses: float32 [2, 384, 384], P('fac'), may hold values from -2 to 2, as said below
- structure: int32 [2, 2], replicated, may hold values 0 or 1
- heater_wattages: bfloat16 [256, 1024], P(None, 'rhs'), may hold values from -0.25 to 0.25
Outputs:
- unknown_vector_results: bfloat16 [1024, 768], P('rhs', 'fac')
- thermal_field_reply: float32 [256, 768], P('rhs', 'fac')
Inputs may be any that keep to these rules, and one draw needn't show every extreme that they name: Each inverses[s] is lower triangular with its diagonal between 0.5 and 2.
All inputs are finite; a program needn't handle non-finite values.
Results may differ from a plain program's by a relative error of at most 0.0095.
Values may be sent and summed in bfloat16 or wider, within the bound.
A program may use at most 64 MiB of HBM per device.

v0:
```python
import jax
import jax.numpy as jnp
from jax import lax
from jax.sharding import PartitionSpec as P


def against_rows(left, right):
    return lax.dot_general(
        left, right, (((1,), (1,)), ((), ())), preferred_element_type=jnp.float32
    )


def body(right_sides, stripe, inverses, structure, heater_wattages):
    block_width = inverses.shape[1]
    supers_count = lax.axis_size("fac")
    resident_position = lax.axis_index("fac")
    right_hand_count = right_sides.shape[0]
    total_rows = block_width * supers_count
    stripe_rows, all_sides = (
        lax.all_gather(stripe, "fac", axis=0, tiled=True),
        lax.all_gather(right_sides, "fac", axis=1, tiled=True),
    )
    every_block_inverse = lax.all_gather(inverses, "fac", axis=0, tiled=True)
    whole = lax.all_gather(stripe_rows, "rhs", axis=1, tiled=True)
    forward_sweep = jnp.zeros((right_hand_count, total_rows), jnp.bfloat16)
    for block in range(supers_count):
        low = block * block_width
        col_mask = jnp.repeat(structure[block], block_width).astype(jnp.bfloat16)
        update = against_rows(forward_sweep * col_mask, whole[low : low + block_width])
        remainder = all_sides[:, low : low + block_width].astype(jnp.float32) - update
        finished_unknowns = jnp.dot(
            remainder, every_block_inverse[block].T, precision=lax.Precision.HIGHEST
        )
        forward_sweep = forward_sweep.at[:, low : low + block_width].set(
            finished_unknowns.astype(jnp.bfloat16)
        )
    unknown_vector_results = jnp.zeros((right_hand_count, total_rows), jnp.bfloat16)
    for block in range(supers_count - 1, -1, -1):
        low = block * block_width
        row_mask = jnp.repeat(structure[:, block], block_width).astype(jnp.bfloat16)
        update = jnp.dot(
            unknown_vector_results * row_mask,
            whole[:, low : low + block_width],
            preferred_element_type=jnp.float32,
        )
        remainder = forward_sweep[:, low : low + block_width].astype(jnp.float32) - update
        finished_unknowns = jnp.dot(
            remainder, every_block_inverse[block], precision=lax.Precision.HIGHEST
        )
        unknown_vector_results = unknown_vector_results.at[:, low : low + block_width].set(
            finished_unknowns.astype(jnp.bfloat16)
        )
    resident_panel = lax.dynamic_slice_in_dim(
        unknown_vector_results, resident_position * block_width, block_width, 1
    )
    thermal_field_reply = lax.psum_scatter(
        jnp.dot(heater_wattages, resident_panel, preferred_element_type=jnp.float32),
        "rhs",
        scatter_dimension=0,
        tiled=True,
    )
    return (resident_panel, thermal_field_reply)


def solution(mesh):
    placed = (P("rhs", "fac"), P("fac", "rhs"), P("fac", None, None), P(), P(None, "rhs"))
    return jax.shard_map(
        body,
        mesh=mesh,
        in_specs=placed,
        out_specs=(P("rhs", "fac"), P("rhs", "fac")),
        check_vma=False,
    )
```

profile of v0, /device:TPU:0, one launch (start us, length us, event | category | flops | bytes accessed | tf_op | source)
XLA Modules:
  0.0 146.0 jit_solution(7706581156529776256)
XLA Ops:
  7.2 0.0 copy-start
  7.2 0.0 all-gather.3.cloned.1.call-start
  7.2 7.3 %all_gather.13 = bf16[768,48]{0,1:T(8,128)(2,1)} all-gather(bf16[384,48]{0,1:T(8,128)(2,1)} %param.14), channel_id=1, replica_groups=mesh['rhs'=16,'fac'=2] {'fac'}, dimensions={0}, use_global_device_ids=true | all-gather | bytes 110592 | tf_op jit(solution)/shard_map/all_gather | solution.py:20
  14.5 0.0 all-gather.3.cloned.1.call-update
  14.5 0.0 all-gather.5.cloned.1.call-start
  14.6 0.7 all-gather.5.cloned.1.call-update
  15.3 0.0 reduce-scatter.4.cloned.1.call-start
  15.3 0.7 convert.6
  16.0 0.1 broadcast_in_dim.16
  16.1 0.1 broadcast_in_dim.17
  16.2 0.2 slice_reduce_fusion
  16.4 0.1 broadcast_in_dim.18
  16.5 0.1 broadcast_in_dim.19
  16.6 0.6 compare_reduce_fusion
  17.2 5.0 %all_gather.12 = bf16[64,768]{1,0:T(8,128)(2,1)S(1)} all-gather(bf16[64,384]{1,0:T(8,128)(2,1)} %param.13), channel_id=1, replica_groups=mesh['rhs'=16,'fac'=2] {'fac'}, dimensions={1}, use_global_device_ids=true | all-gather | bytes 147456 | tf_op jit(solution)/shard_map/all_gather | solution.py:21
  22.2 31.3 %all-gather.3.cloned.1.call-done = bf16[768,768]{0,1:T(8,128)(2,1)} async-done(((bf16[768,48]{0,1:T(8,128)(2,1)}), bf16[768,768]{0,1:T(8,128)(2,1)}) %all-gather.3.cloned.1.call-update) | async-done | bytes 1179664 | tf_op jit(solution)/shard_map/all_gather | solution.py:24
  53.4 1.4 convolution_subtract_fusion.3
  54.8 21.9 %all-gather.5.cloned.1.call-done = f32[2,384,384]{2,1,0:T(8,128)} async-done(((f32[1,384,384]{2,1,0:T(8,128)}), f32[2,384,384]{2,1,0:T(8,128)}) %all-gather.5.cloned.1.call-update) | async-done | bytes 1179664 | tf_op jit(solution)/shard_map/all_gather | solution.py:23
  76.7 2.5 %fusion.1 = bf16[64,384]{1,0:T(8,128)(2,1)S(1)} fusion(f32[64,384]{1,0:T(8,128)S(1)} %convolution_subtract_fusion.3, f32[2,384,384]{2,1,0:T(8,128)} %all-gather.5.cloned.1.call-done, pred[]{:T(512)} %compare_reduce_fusion), kind=kOutput, calls=%fused_computation.10 | convolution fusion | flops 113295360 | bytes 737792 | tf_op jit(solution)/shard_map/dot_general | solution.py:31
  79.3 0.0 copy-done.2
  79.3 0.2 convolution_subtract_fusion.2
  79.5 0.0 copy-done.1
  79.5 0.7 fusion
  80.3 0.3 convolution_subtract_fusion.1
  80.6 0.5 convolution_convert_fusion.1
  81.1 0.3 convolution_subtract_fusion
  81.4 1.1 fusion.2
  82.5 0.0 copy-start.3
  82.5 0.2 convolution_bitcast_fusion
  82.8 0.9 copy.9
  83.7 0.0 reduce-scatter.4.cloned.1.call-update
  83.7 55.7 %reduce-scatter.4.cloned.1.call-done = f32[16,384]{1,0:T(8,128)} async-done(((f32[256,384]{1,0:T(8,128)}), f32[16,384]{1,0:T(8,128)}) %reduce-scatter.4.cloned.1.call-update) | async-done | bytes 24592
  (10 shorter events, 0.1 us)
Async XLA Ops:
  7.2 75.4 %copy-start = (bf16[256,64]{0,1:T(8,128)(2,1)S(1)}, bf16[256,64]{0,1:T(8,128)(2,1)}, u32[]{:S(2)}) copy-start(bf16[256,64]{0,1:T(8,128)(2,1)} %param.17) | copy-start | bytes 98308
  7.2 46.2 %all-gather.3.cloned.1.call-start = ((), (), s32[]{:S(2)}) async-start(), calls=%async_computation.1 | async-start | bytes 1253376 | tf_op jit(solution)/shard_map/all_gather | solution.py:24
  14.5 62.2 %all-gather.5.cloned.1.call-start = ((), (), s32[]{:S(2)}) async-start(), calls=%async_computation.2 | async-start | bytes 1769472 | tf_op jit(solution)/shard_map/all_gather | solution.py:23
  15.3 124.2 %reduce-scatter.4.cloned.1.call-start = ((), (), s32[]{:S(2)}) async-start(), calls=%async_computation.3 | async-start | bytes 417792
  53.4 25.9 %copy-start.2 = (bf16[768,768]{0,1:T(8,128)(2,1)S(1)}, bf16[768,768]{0,1:T(8,128)(2,1)}, u32[]{:S(2)}) copy-start(bf16[768,768]{0,1:T(8,128)(2,1)} %all-gather.3.cloned.1.call-done) | copy-start | bytes 3538948
  76.7 2.8 %copy-start.1 = (f32[2,384,384]{2,1,0:T(8,128)S(1)}, f32[2,384,384]{2,1,0:T(8,128)}, u32[]{:S(2)}) copy-start(f32[2,384,384]{2,1,0:T(8,128)} %all-gather.5.cloned.1.call-done) | copy-start | bytes 3538948
  82.5 56.9 %copy-start.3 = (bf16[64,384]{1,0:T(8,128)(2,1)}, bf16[64,384]{1,0:T(8,128)(2,1)S(1)}, u32[]{:S(2)}) copy-start(bf16[64,384]{1,0:T(8,128)(2,1)S(1)} %fusion.11) | copy-start | bytes 147460
Sparse Core Ops, SparseCore 0:
  14.6 38.7 all-gather.2
  55.0 21.7 all-gather.4
  83.9 55.5 reduce-scatter.3
where the time goes:
time: 146 us
  waiting for transfers between devices  110 us (75%)
  between operations  13.8 us (9%)
  blocking collectives  12.2 us (8%)
  matrix products  7.3 us (5%)
  other arithmetic  1.55 us (1%)
    unnamed x4, waiting for transfers between devices  56.4 us
    all_gather x1, waiting for transfers between devices, body(): whole = lax.all_gather(stripe_rows, 'rhs', axis=1, tiled=True)  31.3 us
    all_gather x1, waiting for transfers between devices, body(): every_block_inverse = lax.all_gather(inverses, 'fac', axis=0, tiled=True)  21.9 us
    all_gather x1, blocking collectives, body(): lax.all_gather(stripe, 'fac', axis=0, tiled=True)  7.25 us
    all_gather x1, blocking collectives, body(): lax.all_gather(right_sides, 'fac', axis=1, tiled=True)  4.97 us
    dot_general x2, matrix products, body(): jnp.dot(remainder, every_block_inverse[block].T, precision=lax.Precision....  3.28 us
  transfers between devices with their start and end apart: 3, of which 3 were waited for; matrix products, arithmetic and copies ran while one was open for 2% of the time, Pallas kernels for 0%

commit v1 on v0

--- a/solution.py
+++ b/solution.py
@@ -2,6 +2,28 @@
 import jax.numpy as jnp
 from jax import lax
 from jax.sharding import PartitionSpec as P
+
+
+def joined_along(blocks, dim):
+    lengths = list(blocks.shape[1:])
+    lengths[dim] *= blocks.shape[0]
+    return jnp.moveaxis(blocks, 0, dim).reshape(lengths)
+
+
+def doubled(shard, axis):
+    peers = lax.axis_size(axis)
+    parts = shard[None]
+    for level in range(peers.bit_length() - 1):
+        distance = 1 << level
+        other = lax.ppermute(parts, axis, [(i, i ^ distance) for i in range(peers)])
+        both = jnp.stack([parts, other])
+        upper = lax.axis_index(axis) >> level & 1
+        parts = jnp.where(upper == 0, both, both[::-1]).reshape(-1, *shard.shape)
+    return parts
+
+
+def gather_by_bits(x, axis, dim):
+    return joined_along(doubled(x, axis), dim)
 
 
 def against_rows(left, right):
@@ -20,7 +42,7 @@
         lax.all_gather(stripe, "fac", axis=0, tiled=True),
         lax.all_gather(right_sides, "fac", axis=1, tiled=True),
     )
-    every_block_inverse = lax.all_gather(inverses, "fac", axis=0, tiled=True)
+    every_block_inverse = gather_by_bits(inverses, "fac", 0)
     whole = lax.all_gather(stripe_rows, "rhs", axis=1, tiled=True)
     forward_sweep = jnp.zeros((right_hand_count, total_rows), jnp.bfloat16)
     for block in range(supers_count):

time: 146 us -> 122 us (0.84)
  waiting for transfers between devices: 110 us -> 76.7 us
  blocking collectives: 12.2 us -> 20.2 us
    all_gather x1 -> x0, waiting for transfers between devices: 21.9 us -> none  [body(): every_block_inverse = lax.all_gather(inverses, 'fac', axis=0, tiled=True)]
    all_gather x1, waiting for transfers between devices: 31.3 us -> 22 us  [body(): whole = lax.all_gather(stripe_rows, 'rhs', axis=1, tiled=True)]
    all_gather x1, blocking collectives: 4.97 us -> 12.9 us  [body(): lax.all_gather(right_sides, 'fac', axis=1, tiled=True)]
    unnamed x4 -> x3, waiting for transfers between devices: 56.4 us -> 54.7 us
  transfers between devices with their start and end apart: 3 -> 3, of which waited for: 3 -> 2; matrix products, arithmetic and copies ran while one was open for 2% -> 3% of each run, Pallas kernels for 0% -> 0%
where the time goes in v1:
time: 122 us
  waiting for transfers between devices  76.7 us (63%)
  blocking collectives  20.2 us (17%)
  between operations  14.1 us (12%)
  matrix products  6.13 us (5%)
  other arithmetic  2.77 us (2%)
  local copies, waits for them, and re-layouts  1.3 us (1%)
    unnamed x3, waiting for transfers between devices  54.7 us
    all_gather x1, waiting for transfers between devices, body(): whole = lax.all_gather(stripe_rows, 'rhs', axis=1, tiled=True)  22 us
    all_gather x1, blocking collectives, body(): lax.all_gather(right_sides, 'fac', axis=1, tiled=True)  12.9 us
    all_gather x1, blocking collectives, body(): lax.all_gather(stripe, 'fac', axis=0, tiled=True)  7.25 us
  transfers between devices with their start and end apart: 3, of which 2 were waited for; matrix products, arithmetic and copies ran while one was open for 3% of the time, Pallas kernels for 0%

profile of v1, /device:TPU:0, one launch (start us, length us, event | category | flops | bytes accessed | tf_op | source)
XLA Modules:
  0.0 122.1 jit_solution(14752444318986038549)
XLA Ops:
  7.2 0.0 copy-start
  7.2 0.0 all-gather.2.cloned.1.call-start
  7.2 7.3 %all_gather.10 = bf16[768,48]{0,1:T(8,128)(2,1)} all-gather(bf16[384,48]{0,1:T(8,128)(2,1)} %param.14), channel_id=1, replica_groups=mesh['rhs'=16,'fac'=2] {'fac'}, dimensions={0}, use_global_device_ids=true | all-gather | bytes 110592 | tf_op jit(solution)/shard_map/all_gather | solution.py:42
  14.5 0.0 all-gather.2.cloned.1.call-update
  14.5 0.0 reduce-scatter.4.cloned.1.call-start
  14.6 0.7 collective-permute-start
  15.3 0.7 convert.6
  16.0 0.1 broadcast_in_dim.19
  16.1 0.1 broadcast_in_dim.21
  16.2 0.2 slice_reduce_fusion
  16.3 0.1 broadcast_in_dim.22
  16.4 0.1 broadcast_in_dim.23
  16.5 0.6 compare_reduce_fusion
  17.2 12.9 %all_gather.9 = bf16[64,768]{1,0:T(8,128)(2,1)S(1)} all-gather(bf16[64,384]{1,0:T(8,128)(2,1)} %param.13), channel_id=1, replica_groups=mesh['rhs'=16,'fac'=2] {'fac'}, dimensions={1}, use_global_device_ids=true | all-gather | bytes 147456 | tf_op jit(solution)/shard_map/all_gather | solution.py:43
  30.1 0.0 collective-permute-done
  30.1 1.1 pad_maximum_fusion
  31.2 0.1 reverse_select_fusion
  31.3 22.0 %all-gather.2.cloned.1.call-done = bf16[768,768]{0,1:T(8,128)(2,1)} async-done(((bf16[768,48]{0,1:T(8,128)(2,1)}), bf16[768,768]{0,1:T(8,128)(2,1)}) %all-gather.2.cloned.1.call-update) | async-done | bytes 1179664 | tf_op jit(solution)/shard_map/all_gather | solution.py:46
  53.4 1.4 %convolution_subtract_fusion.3 = f32[64,384]{1,0:T(8,128)S(1)} fusion(bf16[768,768]{0,1:T(8,128)(2,1)} %all-gather.2.cloned.1.call-done, bf16[64,768]{1,0:T(8,128)(2,1)S(1)} %all_gather.9, bf16[768]{0:T(1024)(128)(2,1)S(1)} %mul_broadcast_in_dim.24), kind=kOutput, calls=%fused_computation.6 | convolution fusion | flops 37797888 | bytes 738816 | tf_op jit(solution)/shard_map/dot_general | solution.py:30
  54.8 1.4 %fusion.1 = bf16[64,384]{1,0:T(8,128)(2,1)S(1)} fusion(f32[64,384]{1,0:T(8,128)S(1)} %convolution_subtract_fusion.3, f32[2,1,1,384,384]{4,3,2,1,0:T(8,128)S(1)} %reverse_select_fusion, pred[]{:T(512)} %compare_reduce_fusion), kind=kOutput, calls=%fused_computation.12 | convolution fusion | flops 113295360 | bytes 737281 | tf_op jit(solution)/shard_map/dot_general | solution.py:53
  56.2 0.2 convolution_subtract_fusion.2
  56.4 0.7 fusion
  57.1 0.3 convolution_subtract_fusion.1
  57.4 0.5 convolution_convert_fusion.1
  57.9 0.3 convolution_subtract_fusion
  58.2 1.1 fusion.2
  59.4 0.0 copy-done
  59.4 0.0 copy-start.2
  59.4 0.2 convolution_bitcast_fusion
  59.6 0.9 copy.9
  60.5 0.0 reduce-scatter.4.cloned.1.call-update
  60.6 54.7 %reduce-scatter.4.cloned.1.call-done = f32[16,384]{1,0:T(8,128)} async-done(((f32[256,384]{1,0:T(8,128)}), f32[16,384]{1,0:T(8,128)}) %reduce-scatter.4.cloned.1.call-update) | async-done | bytes 24592
  (9 shorter events, 0.1 us)
Async XLA Ops:
  7.2 52.2 %copy-start = (bf16[256,64]{0,1:T(8,128)(2,1)S(1)}, bf16[256,64]{0,1:T(8,128)(2,1)}, u32[]{:S(2)}) copy-start(bf16[256,64]{0,1:T(8,128)(2,1)} %param.17) | copy-start | bytes 98308
  7.2 46.2 %all-gather.2.cloned.1.call-start = ((), (), s32[]{:S(2)}) async-start(), calls=%async_computation.1 | async-start | bytes 1253376 | tf_op jit(solution)/shard_map/all_gather | solution.py:46
  14.5 100.7 %reduce-scatter.4.cloned.1.call-start = ((), (), s32[]{:S(2)}) async-start(), calls=%async_computation.2 | async-start | bytes 417792
  14.6 15.5 %collective-permute-start = (f32[1,1,384,384]{3,2,1,0:T(8,128)}, f32[1,1,384,384]{3,2,1,0:T(8,128)S(1)}, u32[]{:S(2)}, u32[]{:S(2)}) collective-permute-start(f32[1,1,384,384]{3,2,1,0:T(8,128)} %bitcast.24), channel_id=1, source_target_pairs={{0,1},{1,0},{2,3},{3,2},{4,5},{5,4},{6,7},{7,6},{8,9},{9,8},{10,11... | collective-permute-start | bytes 1769480 | tf_op jit(solution)/shard_map/ppermute | solution.py:18
  53.4 2.8 %copy-start.1 = (bf16[768,768]{0,1:T(8,128)(2,1)S(1)}, bf16[768,768]{0,1:T(8,128)(2,1)}, u32[]{:S(2)}) copy-start(bf16[768,768]{0,1:T(8,128)(2,1)} %all-gather.2.cloned.1.call-done) | copy-start | bytes 3538948
  59.4 55.8 %copy-start.2 = (bf16[64,384]{1,0:T(8,128)(2,1)}, bf16[64,384]{1,0:T(8,128)(2,1)S(1)}, u32[]{:S(2)}) copy-start(bf16[64,384]{1,0:T(8,128)(2,1)S(1)} %fusion.11) | copy-start | bytes 147460
Sparse Core Ops, SparseCore 0:
  14.6 38.6 all-gather.1
  60.7 54.4 reduce-scatter.3
